TPU v7x, 32 devices: a whole 2x2x4 slice. The times are simulated.
32 devices in a mesh: section: 2 (over core), dp: 4 (over z), ctx: 4 (over y, x).
Axes of the slice: x: 2, y: 2, z: 4, core: 2. Of those that a mesh axis runs over, the one named last changes fastest.
Arguments:
- tokens: bfloat16 [2, 2048, 768], P(None, ('dp', 'ctx')), may hold values from -6 to 6
- cotangent: bfloat16 [2, 2048, 768], P(None, ('dp', 'ctx')), may hold values from -6 to 6
- seq_bound: int32 [4, 2], P('dp'), may hold values from 0 to 448, as said below
- ln1_gain: float32 [2, 768], P('section'), may hold values from 0.5 to 1.5
- ln1_shift: float32 [2, 768], P('section'), may hold values from -1.5 to 1.5
- w_qkv: bfloat16 [2, 768, 2304], P('section'), may hold values from -0.21875 to 0.21875
- w_out: bfloat16 [2, 768, 768], P('section'), may hold values from -3.5 to 3.5
- ln2_gain: float32 [2, 768], P('section'), may hold values from 0.5 to 1.5
- ln2_shift: float32 [2, 768], P('section'), may hold values from -1.5 to 1.5
- w_up: bfloat16 [2, 768, 3072], P('section'), may hold values from -0.21875 to 0.21875
- w_down: bfloat16 [2, 3072, 768], P('section'), may hold values from -0.3125 to 0.3125
Outputs:
- section_outputs: bfloat16 [2, 2, 2048, 768], P('section', None, ('dp', 'ctx'))
- input_grads: float32 [2, 2, 2048, 768], P('section', None, ('dp', 'ctx'))
- grad_qkv: float32 [2, 1769472], P('section', ('dp', 'ctx'))
- grad_out: float32 [2, 589824], P('section', ('dp', 'ctx'))
- grad_up: float32 [2, 2359296], P('section', ('dp', 'ctx'))
- grad_down: float32 [2, 2359296], P('section', ('dp', 'ctx'))
- grad_norms: float32 [2, 3072], P('section', ('dp', 'ctx'))
Inputs may be any that keep to these rules, and one draw needn't show every extreme that they name: `seq_bound`: in every row of slot groups one micro-batch, drawn at random, holds 0, so that its slot is one sequence of 512 positions; every other entry lies between half of 128 and 512 minus half of 128, and some entry equals the latter.
All inputs are finite; a program needn't handle non-finite values.
Results may differ from a plain program's by a relative error of at most 0.023.
Values may be sent and summed in bfloat16 or wider, within the bound.
No kernel may reach another device: no remote copies, remote signals or barrier semaphores. Data moves between devices by JAX's collectives and lax.ppermute only.
A program may use at most 192 MiB of HBM per device.

v0:
```python
import math

import jax
import jax.numpy as jnp
from jax import lax
from jax.sharding import PartitionSpec as P

HEAD_DIM = 64


epsilon = 1e-05
rotary_base = 10000.0
masked_score = -1e30


def shortened(value):
    return jax.tree.map(lambda a: a.astype(jnp.bfloat16) if a.dtype == jnp.float32 else a, value)


def shifted(value, axis, steps):
    count = lax.axis_size(axis)
    leading, last = (max(0, -steps), min(count, count - steps))
    return lax.ppermute(value, axis, [(source, source + steps) for source in range(leading, last)])


def frequencies():
    freq_steps = jnp.arange(HEAD_DIM // 2, dtype=jnp.float32)
    return jnp.exp(-math.log(rotary_base) * 2.0 * freq_steps / HEAD_DIM)


def norm_apply(values, norm_gain, norm_shift):
    centred = values - jnp.mean(values, axis=-1, keepdims=True)
    spread = jnp.mean(centred * centred, axis=-1, keepdims=True)
    return centred * lax.rsqrt(spread + epsilon) * norm_gain + norm_shift


def exact_gelu(inputs):
    return jax.nn.gelu(inputs, approximate=False)


def swap_halves(values):
    row_total, width = values.shape
    parts = values.reshape(row_total, width // HEAD_DIM, 2, HEAD_DIM // 2)
    return parts[:, :, ::-1, :].reshape(row_total, width)


def rotate_flat(values, tables):
    cos_full, sin_signed = tables
    return values * cos_full + swap_halves(values) * sin_signed


def unrotate_flat(values, tables):
    cos_full, sin_signed = tables
    return values * cos_full - swap_halves(values) * sin_signed


def slot_layout(bound_now, ctx_index, row_count, slot_len, model_width):
    local_pos = ctx_index * row_count + jnp.arange(row_count, dtype=jnp.int32)
    every_pos = jnp.arange(slot_len, dtype=jnp.int32)
    seq_local = (local_pos >= bound_now).astype(jnp.int32)
    seq_every = (every_pos >= bound_now).astype(jnp.int32)
    relative = (local_pos - seq_local * bound_now).astype(jnp.float32)
    angles = relative[:, None] * frequencies()[None, :]
    cosine = jnp.cos(angles)
    sine = jnp.sin(angles)
    head_count = model_width // HEAD_DIM
    cos_full = jnp.tile(jnp.concatenate([cosine, cosine], axis=1), (1, head_count))
    sin_signed = jnp.tile(jnp.concatenate([-sine, sine], axis=1), (1, head_count))
    return (seq_local, seq_every, (cos_full, sin_signed))


def fold_step(running, pieces, queries, seq_local, seq_every):
    row_max, row_sum, weighted = running
    key_piece, value_piece = pieces
    count = key_piece.shape[0]
    head_count = queries.shape[1]
    key_piece = key_piece.reshape(count, head_count, HEAD_DIM)
    value_piece = value_piece.reshape(count, head_count, HEAD_DIM)
    same_seq = (seq_local[:, None] == seq_every[None, :])[None]
    scores = jnp.einsum(
        "qhd,khd->hqk", queries, key_piece, preferred_element_type=jnp.float32
    ) * HEAD_DIM ** (-0.5)
    scores = jnp.where(same_seq, scores, masked_score)
    new_max = jnp.maximum(row_max, jnp.max(scores, axis=-1))
    expo = jnp.where(same_seq, jnp.exp(scores - new_max[..., None]), 0.0)
    row_sum = jnp.sum(expo, axis=-1)
    weighted = jnp.einsum(
        "hqk,khd->qhd", expo.astype(jnp.bfloat16), value_piece, preferred_element_type=jnp.float32
    )
    return (new_max, row_sum, weighted)


def forward_layer(layer_input, layer_params, seq_local, seq_every, tables):
    gain_one, shift_one, qkv_weight, out_weight, gain_two, shift_two, up_weight, down_weight = (
        layer_params
    )
    values = layer_input.astype(jnp.float32)
    row_count, model_width = values.shape
    head_count = model_width // HEAD_DIM
    normed = norm_apply(values, gain_one, shift_one).astype(jnp.bfloat16)
    mixed = jnp.dot(normed, qkv_weight, preferred_element_type=jnp.float32)
    queries = rotate_flat(mixed[:, :model_width], tables).astype(jnp.bfloat16)
    keys_local = rotate_flat(mixed[:, model_width : 2 * model_width], tables).astype(jnp.bfloat16)
    values_local = mixed[:, 2 * model_width :].astype(jnp.bfloat16)
    query_heads = queries.reshape(row_count, head_count, HEAD_DIM)
    init = (
        jnp.full((head_count, row_count), masked_score, jnp.float32),
        jnp.zeros((head_count, row_count), jnp.float32),
        jnp.zeros((row_count, head_count, HEAD_DIM), jnp.float32),
    )
    row_max, row_sum, weighted = fold_step(
        init,
        (
            lax.all_gather(keys_local, "ctx", axis=0, tiled=True),
            lax.all_gather(values_local, "ctx", axis=0, tiled=True),
        ),
        query_heads,
        seq_local,
        seq_every,
    )
    attended = weighted / jnp.transpose(row_sum)[:, :, None]
    log_total = row_max + jnp.log(row_sum)
    held = (keys_local, values_local)
    attended_low = attended.reshape(row_count, model_width).astype(jnp.bfloat16)
    hidden = values + jnp.dot(attended_low, out_weight, preferred_element_type=jnp.float32)
    normed_two = norm_apply(hidden, gain_two, shift_two).astype(jnp.bfloat16)
    upward = jnp.dot(normed_two, up_weight, preferred_element_type=jnp.float32)
    active = exact_gelu(upward).astype(jnp.bfloat16)
    result = hidden + jnp.dot(active, down_weight, preferred_element_type=jnp.float32)
    kept = (
        values,
        normed,
        queries,
        held,
        attended_low,
        log_total,
        hidden,
        normed_two,
        upward,
        active,
    )
    return (result, kept)


def weight_grads(operands, norm_grads):
    (
        normed,
        grad_mixed,
        attended_low,
        grad_attn_low,
        normed_two,
        grad_upward,
        active,
        grad_branch,
    ) = operands
    grad_qkv = jnp.einsum("rd,re->de", normed, grad_mixed, preferred_element_type=jnp.float32)
    grad_out = jnp.einsum(
        "rd,re->de", attended_low, grad_attn_low, preferred_element_type=jnp.float32
    )
    grad_up = jnp.einsum("rd,rf->df", normed_two, grad_upward, preferred_element_type=jnp.float32)
    grad_down = jnp.einsum("rf,rd->fd", active, grad_branch, preferred_element_type=jnp.float32)
    return (
        grad_qkv.reshape(-1),
        grad_out.reshape(-1),
        grad_up.reshape(-1),
        grad_down.reshape(-1),
        norm_grads,
    )


def backward_layer(grad_output, kept, layer_params, seq_local, seq_every, tables):
    gain_one, shift_one, qkv_weight, out_weight, gain_two, shift_two, up_weight, down_weight = (
        layer_params
    )
    values, normed, queries, held, attended_low, log_total, hidden, normed_two, upward, active = (
        kept
    )
    row_count, model_width = values.shape
    head_count = model_width // HEAD_DIM
    grad_branch = grad_output.astype(jnp.bfloat16)
    grad_active = jnp.einsum(
        "rd,fd->rf", grad_branch, down_weight, preferred_element_type=jnp.float32
    )
    unused_value, gelu_pull = jax.vjp(exact_gelu, upward)
    grad_upward = gelu_pull(grad_active)[0].astype(jnp.bfloat16)
    grad_normed_two = jnp.einsum(
        "rf,df->rd", grad_upward, up_weight, preferred_element_type=jnp.float32
    )
    unused_norm, norm_pull_two = jax.vjp(norm_apply, hidden, gain_two, shift_two)
    grad_hidden_norm, grad_gain_two, grad_shift_two = norm_pull_two(grad_normed_two)
    grad_hidden = grad_output + grad_hidden_norm
    grad_attn_low = grad_hidden.astype(jnp.bfloat16)
    grad_attended = jnp.einsum(
        "re,de->rd", grad_attn_low, out_weight, preferred_element_type=jnp.float32
    )
    grad_attended = grad_attended.astype(jnp.bfloat16)
    keys_all, values_all = jax.tree.map(
        lambda part, own: part.astype(own.dtype),
        lax.all_gather(shortened(held), "ctx", axis=0, tiled=True),
        held,
    )
    slot_len = keys_all.shape[0]
    key_heads = keys_all.reshape(slot_len, head_count, HEAD_DIM)
    value_heads = values_all.reshape(slot_len, head_count, HEAD_DIM)
    query_heads = queries.reshape(row_count, head_count, HEAD_DIM)
    grad_att_heads = grad_attended.reshape(row_count, head_count, HEAD_DIM)
    same_seq = (seq_local[:, None] == seq_every[None, :])[None]
    scores = jnp.einsum(
        "qhd,khd->hqk", query_heads, key_heads, preferred_element_type=jnp.float32
    ) * HEAD_DIM ** (-0.5)
    probs = jnp.where(same_seq, jnp.exp(scores - log_total[..., None]), 0.0)
    grad_probs = jnp.einsum(
        "qhd,khd->hqk", grad_att_heads, value_heads, preferred_element_type=jnp.float32
    )
    inner_sum = jnp.sum(probs * grad_probs, axis=-1)
    grad_scores = (probs * (grad_probs - inner_sum[..., None])).astype(jnp.bfloat16)
    grad_queries = (
        jnp.einsum("hqk,khd->qhd", grad_scores, key_heads, preferred_element_type=jnp.float32)
        * HEAD_DIM ** (-0.5)
    ).reshape(row_count, model_width)
    grad_values_all = jnp.einsum(
        "hqk,qhd->khd",
        probs.astype(jnp.bfloat16),
        grad_att_heads,
        preferred_element_type=jnp.float32,
    )
    grad_keys_all = jnp.einsum(
        "hqk,qhd->khd", grad_scores, query_heads, preferred_element_type=jnp.float32
    ) * HEAD_DIM ** (-0.5)
    grad_keys, grad_values = (
        lax.psum_scatter(
            grad_keys_all.reshape(slot_len, model_width).astype(jnp.bfloat16),
            "ctx",
            scatter_dimension=0,
            tiled=True,
        ).astype(jnp.float32),
        lax.psum_scatter(
            grad_values_all.reshape(slot_len, model_width).astype(jnp.bfloat16),
            "ctx",
            scatter_dimension=0,
            tiled=True,
        ).astype(jnp.float32),
    )
    grad_query_pre = unrotate_flat(grad_queries, tables)
    grad_key_pre = unrotate_flat(grad_keys, tables)
    grad_mixed = jnp.concatenate([grad_query_pre, grad_key_pre, grad_values], axis=1).astype(
        jnp.bfloat16
    )
    grad_normed = jnp.einsum(
        "re,de->rd", grad_mixed, qkv_weight, preferred_element_type=jnp.float32
    )
    unused_first, norm_pull_one = jax.vjp(norm_apply, values, gain_one, shift_one)
    grad_values_norm, grad_gain_one, grad_shift_one = norm_pull_one(grad_normed)
    grad_input = grad_hidden + grad_values_norm
    operands = (
        normed,
        grad_mixed,
        attended_low,
        grad_attn_low,
        normed_two,
        grad_upward,
        active,
        grad_branch,
    )
    norm_grads = jnp.concatenate([grad_gain_one, grad_shift_one, grad_gain_two, grad_shift_two])
    return (operands, norm_grads, grad_input)


def on_device(
    tokens,
    cotangent,
    seq_bound,
    ln1_gain,
    ln1_shift,
    w_qkv,
    w_out,
    ln2_gain,
    ln2_shift,
    w_up,
    w_down,
):
    section_index = lax.axis_index("section")
    ctx_index = lax.axis_index("ctx")
    ctx_count = lax.axis_size("ctx")
    micro_count, row_count, model_width = tokens.shape
    slot_len = row_count * ctx_count
    first_section = section_index == 0
    layer_params = (
        ln1_gain[0],
        ln1_shift[0],
        w_qkv[0],
        w_out[0],
        ln2_gain[0],
        ln2_shift[0],
        w_up[0],
        w_down[0],
    )
    received = jnp.zeros((row_count, model_width), jnp.bfloat16)
    layouts = []
    saved = []
    results = []
    for step_index in range(micro_count + 1):
        bound_now = jnp.where(
            first_section,
            seq_bound[0, min(step_index, micro_count - 1)],
            seq_bound[0, max(step_index - 1, 0)],
        )
        seq_local, seq_every, tables = slot_layout(
            bound_now, ctx_index, row_count, slot_len, model_width
        )
        layer_input = jnp.where(first_section, tokens[min(step_index, micro_count - 1)], received)
        result, kept = forward_layer(layer_input, layer_params, seq_local, seq_every, tables)
        result_low = result.astype(jnp.bfloat16)
        layouts.append((seq_local, seq_every, tables))
        saved.append(kept)
        results.append(result_low)
        if step_index < micro_count:
            received = shifted(result_low, "section", 1)
    back_received = jnp.zeros((row_count, model_width), jnp.bfloat16)
    input_list = []
    operand_list = []
    norm_total = None
    for turn_index in range(micro_count + 1):
        forward_index = micro_count - turn_index
        if turn_index < micro_count:
            last_grad = cotangent[micro_count - 1 - turn_index]
        else:
            last_grad = jnp.zeros((row_count, model_width), jnp.bfloat16)
        incoming = jnp.where(first_section, back_received, last_grad).astype(jnp.float32)
        seq_local, seq_every, tables = layouts[forward_index]
        operands, norm_grads, grad_input = backward_layer(
            incoming, saved[forward_index], layer_params, seq_local, seq_every, tables
        )
        operand_list.append(operands)
        norm_total = norm_grads if norm_total is None else norm_total + norm_grads
        input_list.append(grad_input)
        if turn_index < micro_count:
            back_received = shifted(grad_input.astype(jnp.bfloat16), "section", -1)
    combined = tuple(
        (
            jnp.where(
                first_section,
                jnp.concatenate(
                    [operand_list[turn][member] for turn in range(1, micro_count + 1)], axis=0
                ),
                jnp.concatenate(
                    [operand_list[turn][member] for turn in range(micro_count)], axis=0
                ),
            )
            for member in range(len(operand_list[0]))
        )
    )
    shares = lax.psum_scatter(
        weight_grads(combined, norm_total), ("dp", "ctx"), scatter_dimension=0, tiled=True
    )
    outputs_first = jnp.stack(results[:micro_count])
    outputs_second = jnp.stack(results[1:])
    section_outputs = jnp.where(first_section, outputs_first, outputs_second)[None]
    grads_first = jnp.stack([input_list[micro_count - index] for index in range(micro_count)])
    grads_second = jnp.stack([input_list[micro_count - 1 - index] for index in range(micro_count)])
    input_grads = jnp.where(first_section, grads_first, grads_second)[None]
    return (
        section_outputs,
        input_grads,
        shares[0][None],
        shares[1][None],
        shares[2][None],
        shares[3][None],
        shares[4][None],
    )


def solution(mesh):
    in_specs = (
        P(None, ("dp", "ctx"), None),
        P(None, ("dp", "ctx"), None),
        P("dp", None),
        P("section", None),
        P("section", None),
        P("section", None, None),
        P("section", None, None),
        P("section", None),
        P("section", None),
        P("section", None, None),
        P("section", None, None),
    )
    out_specs = (
        P("section", None, ("dp", "ctx"), None),
        P("section", None, ("dp", "ctx"), None),
        P("section", ("dp", "ctx")),
        P("section", ("dp", "ctx")),
        P("section", ("dp", "ctx")),
        P("section", ("dp", "ctx")),
        P("section", ("dp", "ctx")),
    )
    return jax.shard_map(
        on_device, mesh=mesh, in_specs=in_specs, out_specs=out_specs, check_vma=False
    )
```

profile of v0, /device:TPU:0, one launch (start us, length us, event | category | flops | bytes accessed | tf_op | source)
XLA Modules:
  0.0 1259.3 jit_solution(174202739982949041)
XLA Ops:
  33.1 15.1 %all_gather.24 = bf16[512,768]{1,0:T(8,128)(2,1)} all-gather(bf16[128,768]{1,0:T(8,128)(2,1)} %slice.112), channel_id=1, replica_groups=mesh['section'=2,'dp'=4,'ctx'=4] {'ctx'}, dimensions={0}, use_global_device_ids=true | all-gather | bytes 983040 | tf_op jit(solution)/shard_map/all_gather | solution.py:115
  65.9 12.4 all_gather.25
  89.2 5.1 multiply_convert_fusion.8
  123.6 11.3 all_gather.26
  152.6 11.8 all_gather.27
  173.4 5.1 multiply_convert_fusion.7
  186.2 12.7 %all_gather.28 = bf16[512,768]{1,0:T(8,128)(2,1)} all-gather(bf16[128,768]{1,0:T(8,128)(2,1)S(1)} %slice.110), channel_id=1, replica_groups=mesh['section'=2,'dp'=4,'ctx'=4] {'ctx'}, dimensions={0}, use_global_device_ids=true | all-gather | bytes 983040 | tf_op jit(solution)/shard_map/all_gather | solution.py:115
  216.7 12.3 all_gather.29
  237.9 4.8 multiply_convert_fusion.6
  272.5 15.4 %reduce-scatter.19.cloned.1.call-done = bf16[128,768]{1,0:T(8,128)(2,1)} async-done(((bf16[512,768]{1,0:T(8,128)(2,1)}), bf16[128,768]{1,0:T(8,128)(2,1)}) %reduce-scatter.19.cloned.1.call-update) | async-done | bytes 196624
  293.5 23.3 %reduce-scatter.21.cloned.1.call-done = bf16[128,768]{1,0:T(8,128)(2,1)} async-done(((bf16[512,768]{1,0:T(8,128)(2,1)}), bf16[128,768]{1,0:T(8,128)(2,1)}) %reduce-scatter.21.cloned.1.call-update) | async-done | bytes 196624
  326.7 4.8 add_convert_fusion.1
  359.2 15.3 %reduce-scatter.23.cloned.1.call-done = bf16[128,768]{1,0:T(8,128)(2,1)} async-done(((bf16[512,768]{1,0:T(8,128)(2,1)}), bf16[128,768]{1,0:T(8,128)(2,1)}) %reduce-scatter.23.cloned.1.call-update) | async-done | bytes 196624
  380.2 23.2 %reduce-scatter.25.cloned.1.call-done = bf16[128,768]{1,0:T(8,128)(2,1)} async-done(((bf16[512,768]{1,0:T(8,128)(2,1)}), bf16[128,768]{1,0:T(8,128)(2,1)}) %reduce-scatter.25.cloned.1.call-update) | async-done | bytes 196624
  413.2 4.8 add_convert_fusion
  457.8 3.7 convolution_bitcast_fusion
  461.6 5.9 copy.149
  467.5 5.1 fusion.59
  472.6 10.8 reshape.723
  495.6 5.7 fusion.136
  501.3 7.9 reshape.720
  513.2 4.5 fusion.186
  520.1 79.4 %all-reduce.4 = f32[3072]{0:T(1024)} all-reduce(f32[3072]{0:T(1024)} %fusion.311), channel_id=12, replica_groups=mesh['section'=2,'dp'=4,'ctx'=4] {'dp','ctx'}, use_global_device_ids=true, to_apply=%region_55.56.clone | all-reduce | flops 3072 | bytes 24576
  604.0 640.8 %all-reduce.8.cloned.1.call-done = (f32[1769472]{0:T(1024)}, f32[589824]{0:T(1024)}, f32[2359296]{0:T(1024)}, f32[2359296]{0:T(1024)}) async-done(((f32[1769472]{0:T(1024)}, f32[589824]{0:T(1024)}, f32[2359296]{0:T(1024)}, f32[2359296]{0:T(1024)}), (f32[1769472]{0:T(1024)}, f32[589824]{0:T(1024)}, f32[2359296]{0:T(1024)}, f32[2359296]{0:T(1024)})) %all-reduce.8.cloned.1.call-update) | async-done | bytes 28311568
  (607 shorter events, 297.3 us)
Async XLA Ops:
  7.2 12.0 copy-start
  7.2 280.6 %reduce-scatter.19.cloned.1.call-start = ((), (), s32[]{:S(2)}) async-start(), calls=%async_computation.6 | async-start | bytes 983040
  87.7 6.6 copy-start.12
  87.7 6.6 slice-start.10
  94.3 7.0 copy-start.108
  94.4 7.6 copy-start.107
  94.4 7.6 copy-start.61
  95.9 22.5 %collective-permute-start = (bf16[128,768]{1,0:T(8,128)(2,1)}, bf16[128,768]{1,0:T(8,128)(2,1)}, u32[]{:S(2)}, u32[]{:S(2)}) collective-permute-start(bf16[128,768]{1,0:T(8,128)(2,1)} %fusion.174), channel_id=1, source_target_pairs={{0,16},{1,17},{2,18},{3,19},{4,20},{5,21},{6,22},{7,23},{8,24},{9,... | collective-permute-start | bytes 589832 | tf_op jit(solution)/shard_map/ppermute | solution.py:23
  171.5 7.1 copy-start.74
  179.5 2.4 collective-permute-start.1
  237.4 9.5 copy-start.14
  261.3 55.5 %reduce-scatter.21.cloned.1.call-start = ((), (), s32[]{:S(2)}) async-start(), calls=%async_computation.7 | async-start | bytes 983040
  267.4 107.1 %reduce-scatter.23.cloned.1.call-start = ((), (), s32[]{:S(2)}) async-start(), calls=%async_computation.8 | async-start | bytes 983040
  318.6 12.9 %slice-start.6 = ((s8[4718592]{0:T(1024)(128)(4,1)}), s8[4194304]{0:T(1024)(128)(4,1)S(1)}, s32[]{:S(2)}) async-start(s8[4718592]{0:T(1024)(128)(4,1)} %bitcast.389), calls=%async_computation.19 | async-start | bytes 8388608
  323.3 3.3 collective-permute-start.2
  326.6 7.5 copy-start.48
  348.3 55.1 %reduce-scatter.25.cloned.1.call-start = ((), (), s32[]{:S(2)}) async-start(), calls=%async_computation.9 | async-start | bytes 983040
  354.3 129.1 %reduce-scatter.27.cloned.1.call-start = ((), (), s32[]{:S(2)}) async-start(), calls=%async_computation.10 | async-start | bytes 983040
  405.1 12.9 %slice-start.8 = ((s8[4718592]{0:T(1024)(128)(4,1)}), s8[4194304]{0:T(1024)(128)(4,1)S(1)}, s32[]{:S(2)}) async-start(s8[4718592]{0:T(1024)(128)(4,1)} %bitcast.391), calls=%async_computation.21 | async-start | bytes 8388608
  409.8 3.3 collective-permute-start.3
  413.1 7.6 copy-start.54
  434.8 55.1 %reduce-scatter.29.cloned.1.call-start = ((), (), s32[]{:S(2)}) async-start(), calls=%async_computation.11 | async-start | bytes 983040
  440.8 804.1 %all-reduce.8.cloned.1.call-start = ((), (), s32[]{:S(2)}) async-start(), calls=%async_computation.12 | async-start | bytes 56623104
  483.4 8.2 copy-start.124
  (169 other events, 524.2 us)
Sparse Core Ops, SparseCore 0:
  261.4 26.3 reduce-scatter.18
  290.7 26.0 reduce-scatter.20
  348.4 26.0 reduce-scatter.22
  377.2 26.0 reduce-scatter.24
  434.9 26.0 reduce-scatter.26
  463.8 26.0 reduce-scatter.28
  509.4 735.4 all-reduce.7
where the time goes:
time: 1270 us; the launch traced here: 1260 us
  waiting for transfers between devices  722 us (57%)
  local copies, waits for them, and re-layouts  179 us (14%)
  blocking collectives  155 us (12%)
  matrix products  118 us (9%)
  other arithmetic  57.4 us (5%)
  between operations  20.8 us (2%)
    unnamed x14, waiting for transfers between devices  719 us
    unnamed x1, blocking collectives  79.4 us
    unnamed x383, local copies, waits for them, and re-layouts  61.4 us
    all_gather x3, blocking collectives, forward_layer(): lax.all_gather(values_local, 'ctx', axis=0, tiled=True)  39.2 us
    all_gather x3, blocking collectives, forward_layer(): lax.all_gather(keys_local, 'ctx', axis=0, tiled=True)  36.5 us
  transfers between devices with their start and end apart: 11, of which 9 were waited for; matrix products, arithmetic and copies ran while one was open for 10% of the time, Pallas kernels for 0%

commit v1 on v0

v1 whole, which is shorter than its diff:
```python
import functools
import math

import jax
import jax.numpy as jnp
from jax import lax
from jax.experimental import pallas as pl
from jax.experimental.pallas import tpu as pltpu
from jax.sharding import PartitionSpec as P

HEAD_DIM = 64
HALF = HEAD_DIM // 2
GROUP = 4
LANES = 128
WIDE = 2 * LANES

epsilon = 1e-05
rotary_base = 10000.0
masked_score = -1e30
low = jnp.bfloat16
full = jnp.float32

NT = (((1,), (1,)), ((), ()))
TN = (((0,), (0,)), ((), ()))


def mm(a, b):
    return jnp.dot(a, b, preferred_element_type=full)


def mm_nt(a, b):
    return lax.dot_general(a, b, NT, preferred_element_type=full)


def mm_tn(a, b):
    return lax.dot_general(a, b, TN, preferred_element_type=full)


def norm_stats(values):
    mean = jnp.mean(values, axis=-1, keepdims=True)
    centred = values - mean
    spread = jnp.mean(centred * centred, axis=-1, keepdims=True)
    scale = lax.rsqrt(spread + epsilon)
    return centred * scale, scale


def norm_backward(values, gain, grad):
    hat, scale = norm_stats(values)
    grad_gain = jnp.sum(grad * hat, axis=0, keepdims=True)
    grad_shift = jnp.sum(grad, axis=0, keepdims=True)
    inner = grad * gain
    first = jnp.mean(inner, axis=-1, keepdims=True)
    second = jnp.mean(inner * hat, axis=-1, keepdims=True)
    return scale * (inner - first - hat * second), grad_gain, grad_shift


def gelu_both(u):
    bell = jnp.exp(-0.5 * u * u)
    z = jnp.abs(u) * (0.5**0.5)
    t = 1.0 / (1.0 + 0.3275911 * z)
    poly = t * (
        0.254829592 + t * (-0.284496736 + t * (1.421413741 + t * (-1.453152027 + t * 1.061405429)))
    )
    tail = 0.5 * poly * bell
    cdf = jnp.where(u >= 0, 1.0 - tail, tail)
    return u * cdf, cdf + u * bell * (1.0 / math.sqrt(2.0 * math.pi))


class Fetch:
    def __init__(self, own, other, use_own, place, target, sem):
        self.parts = (own, other, use_own, place, target, sem)

    def start(self):
        own, other, use_own, place, target, sem = self.parts

        @pl.when(use_own)
        def _():
            pltpu.make_async_copy(own.at[place], target, sem).start()

        @pl.when(jnp.logical_not(use_own))
        def _():
            pltpu.make_async_copy(other.at[place], target, sem).start()

    def wait(self):
        own, other, use_own, place, target, sem = self.parts
        pltpu.make_async_copy(own.at[place], target, sem).wait()


def lane_index(shape):
    return lax.broadcasted_iota(jnp.int32, shape, 1)


def half_mask(head):
    return ((lane_index((1, WIDE)) & (LANES - 1)) // HALF) == head


def value_mask(head):
    return (lane_index((1, WIDE)) // HEAD_DIM) == head


def keep(values, mask):
    return jnp.where(mask, values, jnp.zeros_like(values))


def attend_kernel(layer, heads, sc, x0, x1, x2, x3, norms, cos, sin, w_own, w_oth, n1, qkv, probs, a0, a1, a2, a3, w, sem):
    rows = x0.shape[0]
    fetch = Fetch(w_own, w_oth, sc[0] == layer, (slice(None), slice(None)), w, sem.at[0])
    fetch.start()
    gain, shift = norms[0:1, :], norms[1:2, :]
    for k, x in enumerate((x0, x1, x2, x3)):
        hat, _ = norm_stats(x[...].astype(full))
        n1[k * rows : (k + 1) * rows, :] = (hat * gain + shift).astype(low)
    fetch.wait()
    for k in range(GROUP):
        here = slice(k * rows, (k + 1) * rows)
        mixed = mm(n1[here, :], w[...])
        c, s = cos[here, :], sin[here, :]
        for part in range(2):
            base = part * WIDE
            v1, v2 = mixed[:, base : base + LANES], mixed[:, base + LANES : base + WIDE]
            qkv[here, base : base + LANES] = (v1 * c - v2 * s).astype(low)
            qkv[here, base + LANES : base + WIDE] = (v2 * c + v1 * s).astype(low)
        qkv[here, 2 * WIDE :] = mixed[:, 2 * WIDE :].astype(low)
    me, bound = sc[1], sc[2]
    length = GROUP * rows
    spot = lax.broadcasted_iota(jnp.int32, (1, length), 1)
    place = jnp.zeros((1, length), jnp.int32)
    for k in range(GROUP):
        place = jnp.where(spot // rows == k, (me ^ k) * rows + spot - k * rows, place)
    seq_col = (place >= bound).astype(jnp.int32)
    for k, out in enumerate((a0, a1, a2, a3)):
        here = slice(k * rows, (k + 1) * rows)
        own = (me ^ k) * rows + lax.broadcasted_iota(jnp.int32, (rows, 1), 0)
        same = (own >= bound).astype(jnp.int32) == seq_col
        total = jnp.zeros((rows, WIDE), full)
        for h in range(heads):
            q = keep(qkv[here, 0:WIDE], half_mask(h))
            scores = mm_nt(q, qkv[:, WIDE : 2 * WIDE]) * (HEAD_DIM**-0.5)
            scores = jnp.where(same, scores, masked_score)
            top = jnp.max(scores, axis=-1, keepdims=True)
            expo = jnp.where(same, jnp.exp(scores - top), 0.0)
            p = (expo * (1.0 / jnp.sum(expo, axis=-1, keepdims=True))).astype(low)
            probs[h, here, :] = p
            total = total + mm(p, keep(qkv[:, 2 * WIDE :], value_mask(h)))
        out[...] = total[:, : heads * HEAD_DIM].astype(low)


def attend_back_kernel(layer, heads, sc, g0, g1, g2, g3, qkv, probs, cos, sin, wo_own, wo_oth, w_own, w_oth, gmixed, p0, p1, p2, p3, wo, w, go, gs, qm, gom, sem):
    rows = g0.shape[0]
    width = heads * HEAD_DIM
    me = sc[1]
    mine = sc[0] == layer
    span = pl.ds(pl.multiple_of(me * width, HEAD_DIM), width)
    fetch_o = Fetch(wo_own, wo_oth, mine, (span, slice(None)), wo, sem.at[0])
    fetch_w = Fetch(w_own, w_oth, mine, (slice(None), slice(None)), w, sem.at[1])
    fetch_o.start()
    fetch_w.start()
    fetch_o.wait()
    length = GROUP * rows
    go[:, LANES:] = jnp.zeros((length, WIDE - LANES), low)
    for k, g in enumerate((g0, g1, g2, g3)):
        go[k * rows : (k + 1) * rows, :width] = mm_nt(g[...], wo[...]).astype(low)
    for k in range(GROUP):
        here = slice(k * rows, (k + 1) * rows)
        total = jnp.zeros((rows, WIDE), full)
        for h in range(heads):
            there = slice(h * length + k * rows, h * length + (k + 1) * rows)
            g = keep(go[here, :], value_mask(h))
            gom[there, :] = g
            qm[there, :] = keep(qkv[here, 0:WIDE], half_mask(h))
            gp = mm_nt(g, qkv[:, 2 * WIDE :])
            p = probs[h, here, :].astype(full)
            inner = jnp.sum(p * gp, axis=-1, keepdims=True)
            grad = (p * (gp - inner)).astype(low)
            gs[there, :] = grad
            total = total + mm(grad, keep(qkv[:, WIDE : 2 * WIDE], half_mask(h)))
        total = total * (HEAD_DIM**-0.5)
        c, s = cos[here, :], sin[here, :]
        v1, v2 = total[:, :LANES], total[:, LANES:]
        gmixed[here, 0:LANES] = (v1 * c + v2 * s).astype(low)
        gmixed[here, LANES:WIDE] = (v2 * c - v1 * s).astype(low)
    for k in range(GROUP):
        here = slice(k * rows, (k + 1) * rows)
        gk = mm_tn(gs[:, here], qm[...]) * (HEAD_DIM**-0.5)
        c, s = cos[here, :], sin[here, :]
        v1, v2 = gk[:, :LANES], gk[:, LANES:]
        gmixed[here, WIDE : WIDE + LANES] = (v1 * c + v2 * s).astype(low)
        gmixed[here, WIDE + LANES : 2 * WIDE] = (v2 * c - v1 * s).astype(low)
        gv = jnp.zeros((rows, WIDE), full)
        for h in range(heads):
            gv = gv + mm_tn(probs[h, :, here], gom[h * length : (h + 1) * length, :])
        gmixed[here, 2 * WIDE :] = gv.astype(low)
    fetch_w.wait()
    for k, out in enumerate((p0, p1, p2, p3)):
        out[...] = mm_nt(gmixed[k * rows : (k + 1) * rows, :], w[...]).astype(low)


class FeedWeights:
    def __init__(self, mine, up_own, up_oth, dn_own, dn_oth, wu, wd, sem, first):
        width = wu.shape[1]
        self.wu, self.wd = wu, wd
        self.up, self.down = [], []
        for j in range(GROUP):
            cut = slice(j * width, (j + 1) * width)
            self.up.append(Fetch(up_own, up_oth, mine, (slice(None), cut), wu.at[j], sem.at[first + j]))
            self.down.append(Fetch(dn_own, dn_oth, mine, (cut, slice(None)), wd.at[j], sem.at[first + GROUP + j]))


def feed_forward(me, x, atts, norms, fetch_o, wo, feed, shards, y, hidden, slope, messages, parts, cols):
    rows, width = x.shape
    heads_wide = atts[0].shape[1]
    for k in range(GROUP):
        fetch_o[k].wait()
    state = x[...].astype(full)
    for k in range(GROUP):
        state = state + mm(atts[k][...], wo[k])
        cols[me ^ k] = atts[k][...]
    hidden[...] = state
    hat, _ = norm_stats(state)
    n2 = (hat * norms[2:3, :] + norms[3:4, :]).astype(low)
    for message in messages:
        message[:, 0:width] = n2
    step = width // (GROUP * shards)
    for target in range(GROUP):
        pieces = []
        for z in range(shards):
            at = (z * GROUP + target) * step
            pieces.append(cols[at // heads_wide, :, at % heads_wide : at % heads_wide + step])
        pieces.append(jnp.zeros((rows, WIDE - heads_wide), low))
        parts[target, :, width : width + WIDE] = jnp.concatenate(pieces, axis=1)
    out = jnp.zeros((rows, width), full)
    chunk = feed.wu.shape[2]
    for j in range(GROUP):
        feed.up[j].wait()
        act, grad = gelu_both(mm(n2, feed.wu[j]))
        act = act.astype(low)
        slope[:, j * chunk : (j + 1) * chunk] = grad.astype(low)
        feed.down[j].wait()
        out = out + mm(act, feed.wd[j])
        span = chunk * GROUP // (GROUP * shards)
        for b in range(chunk // span):
            z, target = divmod(j * (chunk // span) + b, GROUP)
            parts[target, :, z * span : (z + 1) * span] = act[:, b * span : (b + 1) * span]
    y[...] = (hidden[...] + out).astype(low)
    for k, message in enumerate(messages):
        message[:, width : 2 * width + WIDE] = parts[me ^ k]


def feed_back(me, gf, grad_out, norms, feed, hidden, slope, ga, gh, dnorm, messages, offset, gu, waited):
    rows, width = gf.shape
    chunk = feed.wu.shape[2]
    grad = jnp.zeros((rows, width), full)
    for j in range(GROUP):
        if not waited:
            feed.down[j].wait()
        got = mm_nt(gf, feed.wd[j]) * slope[:, j * chunk : (j + 1) * chunk].astype(full)
        got = got.astype(low)
        gu[j] = got
        if not waited:
            feed.up[j].wait()
        grad = grad + mm_nt(got, feed.wu[j])
    back, d_gain, d_shift = norm_backward(hidden[...], norms[2:3, :], grad)
    total = grad_out + back
    gh[...] = total
    ga[...] = total.astype(low)
    dnorm[0:1, :] = d_gain
    dnorm[1:2, :] = d_shift
    for k, message in enumerate(messages):
        message[:, offset : offset + width] = gf
        message[:, offset + width : offset + 2 * width] = gu[me ^ k]


def start_out(sc, mine, wo_own, wo_oth, wo, sem):
    width = wo.shape[1]
    out = []
    for k in range(GROUP):
        span = pl.ds(pl.multiple_of((sc[1] ^ k) * width, HEAD_DIM), width)
        out.append(Fetch(wo_own, wo_oth, mine, (span, slice(None)), wo.at[k], sem.at[k]))
    return out


def feed_kernel(layer, shards, sc, x, a0, a1, a2, a3, norms, wo_own, wo_oth, up_own, up_oth, dn_own, dn_oth, y, hidden, slope, m0, m1, m2, m3, wo, wu, wd, parts, cols, sem):
    mine = sc[0] == layer
    fetch_o = start_out(sc, mine, wo_own, wo_oth, wo, sem)
    feed = FeedWeights(mine, up_own, up_oth, dn_own, dn_oth, wu, wd, sem, GROUP)
    for f in fetch_o + [f for pair in zip(feed.up, feed.down) for f in pair]:
        f.start()
    feed_forward(sc[1], x, (a0, a1, a2, a3), norms, fetch_o, wo, feed, shards, y, hidden, slope, (m0, m1, m2, m3), parts, cols)


def feed_turn_kernel(layer, shards, sc, x, a0, a1, a2, a3, norms, cot, wo_own, wo_oth, up_own, up_oth, dn_own, dn_oth, y, ga, gh, dnorm, m0, m1, m2, m3, wo, wu, wd, parts, cols, hidden, slope, gu, sem):
    mine = sc[0] == layer
    fetch_o = start_out(sc, mine, wo_own, wo_oth, wo, sem)
    feed = FeedWeights(mine, up_own, up_oth, dn_own, dn_oth, wu, wd, sem, GROUP)
    for f in fetch_o + [f for pair in zip(feed.up, feed.down) for f in pair]:
        f.start()
    messages = (m0, m1, m2, m3)
    feed_forward(sc[1], x, (a0, a1, a2, a3), norms, fetch_o, wo, feed, shards, y, hidden, slope, messages, parts, cols)
    gf = cot[...]
    feed_back(sc[1], gf, gf.astype(full), norms, feed, hidden, slope, ga, gh, dnorm, messages, 2 * gf.shape[1] + WIDE, gu, True)


def turn_kernel(layer, sc, r0, r1, r2, r3, gh_in, x_in, norms_in, hidden, slope, norms, up_own, up_oth, dn_own, dn_oth, gx, dnorm_in, ga, gh, dnorm, m0, m1, m2, m3, wu, wd, gu, sem):
    mine = sc[0] == layer
    feed = FeedWeights(mine, up_own, up_oth, dn_own, dn_oth, wu, wd, sem, 0)
    for f in [f for pair in zip(feed.down, feed.up) for f in pair]:
        f.start()
    top = first_norm_back(r0, r1, r2, r3, gh_in, x_in, norms_in, gx, dnorm_in)
    gf = top.astype(low)
    feed_back(sc[1], gf, gf.astype(full), norms, feed, hidden, slope, ga, gh, dnorm, (m0, m1, m2, m3), 0, gu, False)


def first_norm_back(r0, r1, r2, r3, gh_in, x_in, norms_in, gx, dnorm):
    grad = r0[...].astype(full) + r1[...].astype(full) + r2[...].astype(full) + r3[...].astype(full)
    back, d_gain, d_shift = norm_backward(x_in[...].astype(full), norms_in[0:1, :], grad)
    dnorm[0:1, :] = d_gain
    dnorm[1:2, :] = d_shift
    total = gh_in[...] + back
    gx[...] = total
    return total


def last_kernel(r0, r1, r2, r3, gh_in, x_in, norms_in, gx, dnorm):
    first_norm_back(r0, r1, r2, r3, gh_in, x_in, norms_in, gx, dnorm)


def tall_product(left, right, out, step):
    @pl.loop(0, left.shape[1] // step)
    def _(i):
        cut = pl.ds(pl.multiple_of(i * step, step), step)
        out[cut, :] = mm_tn(left[:, cut], right[...]).astype(out.dtype)


def feed_grads_kernel(split, *refs):
    if split:
        fwd, bwd, (g_up, g_down, a, b) = refs[:GROUP], refs[GROUP : 2 * GROUP], refs[2 * GROUP :]
        base = 0
    else:
        fwd, (g_up, g_down, a, b) = refs[:GROUP], refs[GROUP:]
        bwd, base = fwd, 2 * g_up.shape[0] + WIDE
    rows, width = fwd[0].shape[0], g_up.shape[0]
    for k in range(GROUP):
        here = slice(k * rows, (k + 1) * rows)
        a[here, :] = fwd[k][:, 0:width]
        b[here, :] = bwd[k][:, base + width : base + 2 * width]
    tall_product(a, b, g_up, WIDE)
    for k in range(GROUP):
        here = slice(k * rows, (k + 1) * rows)
        a[here, :] = fwd[k][:, width : 2 * width]
        b[here, :] = bwd[k][:, base : base + width]
    tall_product(a, b, g_down, WIDE)


def attend_grads_kernel(n1, gmixed, m0, m1, m2, m3, g0, g1, g2, g3, g_qkv, g_out, a, b):
    rows, width = g0.shape
    tall_product(n1, gmixed, g_qkv, WIDE)
    for k, (m, g) in enumerate(zip((m0, m1, m2, m3), (g0, g1, g2, g3))):
        here = slice(k * rows, (k + 1) * rows)
        a[here, :] = m[:, 2 * width : 2 * width + WIDE]
        b[here, :] = g[...]
    g_out[...] = mm_tn(a[...], b[...])[: g_out.shape[0], :].astype(low)


def run(kernel, shapes, scratch, operands, spaces, flops=0, moved=0):
    place = {"s": pltpu.SMEM, "v": pltpu.VMEM, "a": pl.ANY}
    return pl.pallas_call(
        kernel,
        out_shape=[jax.ShapeDtypeStruct(shape, kind) for shape, kind in shapes],
        in_specs=[pl.BlockSpec(memory_space=place[space]) for space in spaces],
        out_specs=[pl.BlockSpec(memory_space=pltpu.VMEM) for _ in shapes],
        scratch_shapes=scratch,
        compiler_params=pltpu.CompilerParams(vmem_limit_bytes=56 * 2**20),
        cost_estimate=pl.CostEstimate(flops=flops, bytes_accessed=moved, transcendentals=0),
    )(*operands)


def exchange(value):
    values = value if isinstance(value, (list, tuple)) else [value] * GROUP
    return [values[0]] + [
        lax.ppermute(values[k], "ctx", [(i, i ^ k) for i in range(GROUP)]) for k in range(1, GROUP)
    ]


def swap(value):
    return lax.ppermute(value, "section", [(0, 1), (1, 0)])


def rotary_tables(me, bound, rows):
    spot = jnp.arange(GROUP * rows, dtype=jnp.int32)
    place = (me ^ (spot // rows)) * rows + spot % rows
    relative = (place - jnp.where(place >= bound, bound, 0)).astype(full)
    steps = (jnp.arange(LANES, dtype=jnp.int32) % HALF).astype(full)
    freqs = jnp.exp(-math.log(rotary_base) * 2.0 * steps / HEAD_DIM)
    angles = relative[:, None] * freqs[None, :]
    return jnp.cos(angles), jnp.sin(angles)


def chosen_columns(me, width, heads):
    t = jnp.arange(3 * WIDE, dtype=jnp.int32)
    part, u = t // WIDE, t % WIDE
    half, v = u // LANES, u % LANES
    rotated = part * width + (me * heads + v // HALF) * HEAD_DIM + half * HALF + v % HALF
    plain = 2 * width + me * heads * HEAD_DIM + u
    return jnp.where(
        part < 2,
        jnp.where(v < heads * HALF, rotated, -1),
        jnp.where(u < heads * HEAD_DIM, plain, -1),
    )


def along_dp(layer, own, other):
    count = lax.axis_size("dp")
    z = lax.axis_index("dp")
    total = own.astype(full) + other.astype(full)
    blocks = total.reshape((count, total.shape[0] // count) + total.shape[1:])
    if count > 8:
        return lax.psum_scatter(blocks.astype(low), "dp", scatter_dimension=0, tiled=False).astype(full)
    result = lax.dynamic_index_in_dim(blocks, z, 0, keepdims=False)
    for k in range(1, count):
        block = lax.dynamic_index_in_dim(blocks, lax.rem(z + k, count), 0, keepdims=False).astype(low)
        pairs = [(layer * count + i, layer * count + (i + k) % count) for i in range(count)]
        result = result + lax.ppermute(block, ("section", "dp"), pairs).astype(full)
    return result


def on_device(tokens, cotangent, seq_bound, ln1_gain, ln1_shift, w_qkv, w_out, ln2_gain, ln2_shift, w_up, w_down):
    section = lax.axis_index("section")
    me = lax.axis_index("ctx")
    shards = lax.axis_size("dp")
    z = lax.axis_index("dp")
    rows, width = tokens.shape[1:]
    feed_width = w_up.shape[2]
    chunk = feed_width // GROUP
    heads = width // HEAD_DIM // GROUP
    mine_wide = heads * HEAD_DIM
    length = GROUP * rows
    bound = lax.dynamic_index_in_dim(seq_bound[0], section, 0, keepdims=False)
    sc = jnp.stack([section, me, bound]).astype(jnp.int32)

    x = lax.dynamic_index_in_dim(tokens, section, 0, keepdims=False)
    cot = lax.dynamic_index_in_dim(cotangent, section, 0, keepdims=False)
    gathered = exchange(x)

    norms_own = jnp.concatenate([ln1_gain, ln1_shift, ln2_gain, ln2_shift], axis=0)
    norms_oth = swap(norms_own)
    norms = [jnp.where(section == layer, norms_own, norms_oth) for layer in range(2)]
    pick = chosen_columns(me, width, heads)
    select = (jnp.arange(3 * width, dtype=jnp.int32)[:, None] == pick[None, :]).astype(low)
    wq_own = mm(w_qkv[0], select).astype(low)
    wq_oth = swap(wq_own)
    wo_own, up_own, dn_own = w_out[0], w_up[0], w_down[0]
    wo_oth, up_oth, dn_oth = swap(wo_own), swap(up_own), swap(dn_own)
    cos, sin = rotary_tables(me, bound, rows)

    dma = pltpu.SemaphoreType.DMA
    vm = pltpu.VMEM
    piece = ((rows, width), low)

    def attend(layer, gathered):
        return run(
            functools.partial(attend_kernel, layer, heads),
            [((length, width), low), ((length, 3 * WIDE), low), ((heads, length, length), low)] + [((rows, mine_wide), low)] * GROUP,
            [vm((width, 3 * WIDE), low), dma((1,))],
            (sc, *gathered, norms[layer], cos, sin, wq_own, wq_oth),
            "svvvvvvvaa",
            flops=2 * length * width * 3 * WIDE * 2, moved=8 * 2**20,
        )

    def attend_back(layer, grads, qkv, probs):
        return run(
            functools.partial(attend_back_kernel, layer, heads),
            [((length, 3 * WIDE), low)] + [piece] * GROUP,
            [
                vm((mine_wide, width), low), vm((width, 3 * WIDE), low), vm((length, WIDE), low),
                vm((heads * length, length), low), vm((heads * length, WIDE), low), vm((heads * length, WIDE), low), dma((2,)),
            ],
            (sc, *grads, qkv, probs, cos, sin, wo_own, wo_oth, wq_own, wq_oth),
            "svvvvvvvvaaaa",
            flops=2 * length * width * 3 * WIDE * 3, moved=8 * 2**20,
        )

    feed_scratch = [vm((GROUP, width, chunk), low), vm((GROUP, chunk, width), low)]
    out_scratch = vm((GROUP, mine_wide, width), low)
    split_scratch = [vm((GROUP, rows, width + WIDE), low), vm((GROUP, rows, mine_wide), low)]
    weights = (wo_own, wo_oth, up_own, up_oth, dn_own, dn_oth)

    n1_0, qkv_0, probs_0, *att = attend(0, gathered)
    att = exchange(att)
    y0, hidden_0, slope_0, *fwd_0 = run(
        functools.partial(feed_kernel, 0, shards),
        [piece, ((rows, width), full), ((rows, feed_width), low)] + [((rows, 2 * width + WIDE), low)] * GROUP,
        [out_scratch, *feed_scratch, *split_scratch, dma((3 * GROUP,))],
        (sc, x, *att, norms[0], *weights),
        "svvvvvvaaaaaa",
        flops=4 * rows * width * feed_width, moved=14 * 2**20,
    )
    gathered_1 = exchange(y0)
    fwd_0 = exchange(fwd_0)
    n1_1, qkv_1, probs_1, *att = attend(1, gathered_1)
    att = exchange(att)
    y1, ga, gh_1, dn2_1, *both_1 = run(
        functools.partial(feed_turn_kernel, 1, shards),
        [piece, piece, ((rows, width), full), ((2, width), full)] + [((rows, 4 * width + WIDE), low)] * GROUP,
        [
            out_scratch, *feed_scratch, *split_scratch, vm((rows, width), full), vm((rows, feed_width), low),
            vm((GROUP, rows, chunk), low), dma((3 * GROUP,)),
        ],
        (sc, y0, *att, norms[1], cot, *weights),
        "svvvvvvvaaaaaa",
        flops=8 * rows * width * feed_width, moved=14 * 2**20,
    )
    ga_1 = exchange(ga)
    both_1 = exchange(both_1)
    gmixed_1, *back = attend_back(1, ga_1, qkv_1, probs_1)
    back = exchange(back)
    gx_1, dn1_1, ga, gh_0, dn2_0, *bwd_0 = run(
        functools.partial(turn_kernel, 0),
        [((rows, width), full), ((2, width), full), piece, ((rows, width), full), ((2, width), full)]
        + [((rows, 2 * width), low)] * GROUP,
        [*feed_scratch, vm((GROUP, rows, chunk), low), dma((2 * GROUP,))],
        (sc, *back, gh_1, y0, norms[1], hidden_0, slope_0, norms[0], up_own, up_oth, dn_own, dn_oth),
        "svvvvvvvvvvaaaa",
        flops=4 * rows * width * feed_width, moved=12 * 2**20,
    )
    ga_0 = exchange(ga)
    bwd_0 = exchange(bwd_0)
    gmixed_0, *back = attend_back(0, ga_0, qkv_0, probs_0)
    back = exchange(back)
    gx_0, dn1_0 = run(
        last_kernel,
        [((rows, width), full), ((2, width), full)],
        [],
        (*back, gh_0, x, norms[0]),
        "vvvvvvv",
        moved=2**20,
    )

    def grads_of(layer, messages, n1, gmixed, ga):
        square = ((width, width), low)
        stage = [vm((length, width), low), vm((length, width), low)]
        g_up, g_down = run(
            functools.partial(feed_grads_kernel, len(messages) > GROUP),
            [((width, chunk), low), ((chunk, width), low)], stage, messages, "v" * len(messages),
            flops=4 * length * width * chunk, moved=8 * 2**20,
        )
        g_qkv, g_out = run(
            attend_grads_kernel,
            [((width, 3 * WIDE), low), ((mine_wide, width), low)],
            [vm((length, WIDE), low), vm((length, width), low)],
            (n1, gmixed, *messages[:GROUP], *ga), "v" * (2 + 2 * GROUP),
            flops=2 * length * width * width, moved=8 * 2**20,
        )
        totals = []
        for g in (g_up, g_down, g_out, g_qkv):
            other = lax.ppermute(g, "section", [(1 - layer, layer)])
            totals.append(along_dp(layer, g, other))
        return totals

    totals_1 = grads_of(1, both_1, n1_1, gmixed_1, ga_1)
    totals_0 = grads_of(0, fwd_0 + bwd_0, n1_0, gmixed_0, ga_0)
    t_up, t_down, t_out, t_qkv = (
        jnp.where(section == 0, first, second) for first, second in zip(totals_0, totals_1)
    )
    slim = jnp.concatenate([t_up, t_qkv], axis=1).astype(low)
    slim = slim.reshape(GROUP, slim.shape[0] // GROUP, slim.shape[1])
    sends = [lax.dynamic_index_in_dim(slim, me ^ k, 0, keepdims=False) for k in range(GROUP)]
    gets = jnp.stack(exchange(sends))
    gets = jnp.stack([lax.dynamic_index_in_dim(gets, me ^ k, 0, keepdims=False) for k in range(GROUP)]).astype(full)
    few = gets.shape[1]
    grad_up = jnp.transpose(gets[:, :, :chunk], (1, 0, 2)).reshape(1, -1)
    cols = gets[:, :, chunk:].reshape(GROUP, few, 3, WIDE)
    turned = cols[:, :, :2].reshape(GROUP, few, 2, 2, LANES)[..., : heads * HALF]
    turned = turned.reshape(GROUP, few, 2, 2, heads, HALF).transpose(1, 2, 0, 4, 3, 5).reshape(few, 2 * width)
    plain = cols[:, :, 2, :mine_wide].transpose(1, 0, 2).reshape(few, width)
    grad_qkv = jnp.concatenate([turned, plain], axis=1).reshape(1, -1)
    grad_down = t_down.reshape(1, -1)
    grad_out = t_out.reshape(1, -1)

    small = [jnp.concatenate([dn1_0, dn2_0]), jnp.concatenate([dn1_1, dn2_1])]
    small = jnp.where(section == 0, small[0], small[1]) + swap(jnp.where(section == 0, small[1], small[0]))
    small = small.reshape(shards * GROUP, -1)
    grad_norms = lax.psum_scatter(small, ("dp", "ctx"), scatter_dimension=0, tiled=True)

    def by_section(first, second):
        own = jnp.where(section == 0, first, second)
        got = swap(jnp.where(section == 0, second, first))
        return jnp.where(section == 0, jnp.stack([own, got]), jnp.stack([got, own]))[None]

    return (
        by_section(y0, y1),
        by_section(gx_0, gx_1),
        grad_qkv,
        grad_out,
        grad_up,
        grad_down,
        grad_norms,
    )


def solution(mesh):
    in_specs = (
        P(None, ("dp", "ctx"), None),
        P(None, ("dp", "ctx"), None),
        P("dp", None),
        P("section", None),
        P("section", None),
        P("section", None, None),
        P("section", None, None),
        P("section", None),
        P("section", None),
        P("section", None, None),
        P("section", None, None),
    )
    out_specs = (
        P("section", None, ("dp", "ctx"), None),
        P("section", None, ("dp", "ctx"), None),
        P("section", ("dp", "ctx")),
        P("section", ("dp", "ctx")),
        P("section", ("dp", "ctx")),
        P("section", ("dp", "ctx")),
        P("section", ("dp", "ctx")),
    )
    return jax.shard_map(
        on_device, mesh=mesh, in_specs=in_specs, out_specs=out_specs, check_vma=False
    )
```

time: 1270 us -> 471 us (0.37)
  waiting for transfers between devices: 722 us -> 130 us
  local copies, waits for them, and re-layouts: 179 us -> 25.6 us
  starting transfers between devices: 6.51 us -> 126 us
  matrix products: 118 us -> 4.08 us
  Pallas kernels: 0 us -> 86.6 us
  blocking collectives: 155 us -> 76.3 us
  other arithmetic: 57.4 us -> 15.6 us
  between operations: 20.8 us -> 2.19 us
    unnamed x14 -> x0, waiting for transfers between devices: 719 us -> none
    ppermute x4 -> x76, waiting for transfers between devices: 3.12 us -> 130 us  [the longest x36 97.2 us: exchange(): lax.ppermute(values[k], 'ctx', [(i, i ^ k) for i in range(GROUP)])]
    ppermute x4 -> x76, starting transfers between devices: 5.83 us -> 126 us  [the longest x24 57.6 us: along_dp(): result = result + lax.ppermute(block, ('section', 'dp'), pairs).astype(full)]
    dot_general x46 -> x1, matrix products: 118 us -> 4.08 us  [mm(): return jnp.dot(a, b, preferred_element_type=full)]
    pallas_call x0 -> x12, Pallas kernels: none -> 86.6 us  [run(): pl.pallas_call(kernel, out_shape=[jax.ShapeDtypeStruct(shape, kind) for s...]
    all_gather x6 -> x0, blocking collectives: 75.7 us -> none  [the longest x3 39.2 us: forward_layer(): lax.all_gather(values_local, 'ctx', axis=0, tiled=True)]
    unnamed x383 -> x120, local copies, waits for them, and re-layouts: 61.4 us -> 11.1 us
    reshape x9 -> x6, local copies, waits for them, and re-layouts: 33.4 us -> 6.34 us  [the longest x1 2.59 us: on_device(): grad_up = jnp.transpose(gets[:, :, :chunk], (1, 0, 2)).reshape(1, -1)]
  transfers between devices with their start and end apart: 11 -> 76, of which waited for: 9 -> 29; matrix products, arithmetic and copies ran while one was open for 10% -> 6% of each run, Pallas kernels for 0% -> 9%
where the time goes in v1:
time: 471 us; the launch traced here: 466 us
  waiting for transfers between devices  130 us (28%)
  starting transfers between devices  126 us (27%)
  Pallas kernels  86.6 us (18%)
  blocking collectives  76.3 us (16%)
  local copies, waits for them, and re-layouts  25.6 us (5%)
  other arithmetic  15.6 us (3%)
    ppermute x36, waiting for transfers between devices, exchange(): lax.ppermute(values[k], 'ctx', [(i, i ^ k) for i in range(GROUP)])  97.2 us
    pallas_call x12, Pallas kernels, run(): pl.pallas_call(kernel, out_shape=[jax.ShapeDtypeStruct(shape, kind) for s...  86.6 us
    unnamed x1, blocking collectives  76.3 us
    ppermute x24, starting transfers between devices, along_dp(): result = result + lax.ppermute(block, ('section', 'dp'), pairs).astype(full)  57.6 us
    ppermute x36, starting transfers between devices, exchange(): lax.ppermute(values[k], 'ctx', [(i, i ^ k) for i in range(GROUP)])  45.2 us
    ppermute x24, waiting for transfers between devices, along_dp(): result = result + lax.ppermute(block, ('section', 'dp'), pairs).astype(full)  32.5 us
    ppermute x8, starting transfers between devices, grads_of(): other = lax.ppermute(g, 'section', [(1 - layer, layer)])  18.7 us
    unnamed x120, local copies, waits for them, and re-layouts  11.1 us
  transfers between devices with their start and end apart: 76, of which 29 were waited for; matrix products, arithmetic and copies ran while one was open for 6% of the time, Pallas kernels for 9%

profile of v1, /device:TPU:0, one launch (start us, length us, event | category | flops | bytes accessed | tf_op | source)
XLA Modules:
  0.0 465.7 jit_solution(2448068283882513641)
XLA Ops:
  2.7 4.1 fusion.6.w_own
  28.0 3.6 collective-permute-done.2.x3
  32.7 7.8 %shard_map.162 = (bf16[512,768]{1,0:T(8,128)(2,1)}, bf16[512,768]{1,0:T(8,128)(2,1)}, bf16[3,512,512]{2,1,0:T(8,128)(2,1)}, bf16[128,192]{1,0:T(8,128)(2,1)}, bf...) custom-call(s32[3]{0:T(128)} %pad_add_fusion.sc, bf16[128,768]{1,0:T(8,128)(2,1)} %copy-done.5, ...), custom_call_target="tpu_custom_call" | custom-call | flops 1207959552 | bytes 8388608 | tf_op jit(solution)/shard_map/pallas_call | solution.py:366
  49.4 8.0 %shard_map.163 = (bf16[128,768]{1,0:T(8,128)(2,1)}, f32[128,768]{1,0:T(8,128)}, bf16[128,3072]{1,0:T(8,128)(2,1)}, bf16[128,1792]{1,0:T(8,128)(2,1)}, bf16[128,1...) custom-call(s32[3]{0:T(128)} %pad_add_fusion.sc, bf16[128,768]{1,0:T(8,128)(2,1)} %copy-done.5, ...), custom_call_target="tpu_custom_call" | custom-call | flops 1207959552 | bytes 14680064 | tf_op jit(solution)/shard_map/pallas_call | solution.py:366
  66.7 7.8 %shard_map.164 = (bf16[512,768]{1,0:T(8,128)(2,1)}, bf16[512,768]{1,0:T(8,128)(2,1)}, bf16[3,512,512]{2,1,0:T(8,128)(2,1)}, bf16[128,192]{1,0:T(8,128)(2,1)}, bf...) custom-call(s32[3]{0:T(128)} %pad_add_fusion.sc, ...), custom_call_target="tpu_custom_call" | custom-call | flops 1207959552 | bytes 8388608 | tf_op jit(solution)/shard_map/pallas_call | solution.py:366
  82.9 11.7 %shard_map.165 = (bf16[128,768]{1,0:T(8,128)(2,1)}, bf16[128,768]{1,0:T(8,128)(2,1)}, f32[128,768]{1,0:T(8,128)}, f32[2,768]{1,0:T(2,128)}, bf16[128,3328]{1,0:T...) custom-call(s32[3]{0:T(128)} %pad_add_fusion.sc, ...), custom_call_target="tpu_custom_call" | custom-call | flops 2415919104 | bytes 14680064 | tf_op jit(solution)/shard_map/pallas_call | solution.py:366
  104.0 9.1 %shard_map.166 = (bf16[512,768]{1,0:T(8,128)(2,1)}, bf16[128,768]{1,0:T(8,128)(2,1)}, bf16[128,768]{1,0:T(8,128)(2,1)}, bf16[128,768]{1,0:T(8,128)(2,1)}, bf16[128,768]{1,0:T(8,128)(2,1)}) custom-call(s32[3]{0:T(128)} %pad_add_fusion.sc, bf16[128,768]{1,0:T(8,128)(2,1)} %get-tuple-element.75.g0, bf16[128,768]{1,0:T(8,128)(2,1)} %copy-done.13, ...), custom_call_target="tpu_custom_call" | custom-call | flops 1811939328 | bytes 8388608 | tf_op jit(solution)/shard_map/pallas_call | solution.py:366
  123.3 9.5 %shard_map.167 = (f32[128,768]{1,0:T(8,128)}, f32[2,768]{1,0:T(2,128)}, bf16[128,768]{1,0:T(8,128)(2,1)}, f32[128,768]{1,0:T(8,128)}, f32[2,768]{1,0:T(2,128)}, ...) custom-call(s32[3]{0:T(128)} %pad_add_fusion.sc, ...), custom_call_target="tpu_custom_call" | custom-call | flops 1207959552 | bytes 12582912 | tf_op jit(solution)/shard_map/pallas_call | solution.py:366
  142.2 13.1 %collective-permute-done.25.g2 = bf16[128,768]{1,0:T(8,128)(2,1)S(1)} collective-permute-done((bf16[128,768]{1,0:T(8,128)(2,1)}, bf16[128,768]{1,0:T(8,128)(2,1)S(1)}, u32[]{:S(2)}, u32[]{:S(2)}) %collective-permute-start.25) | collective-permute-done | bytes 196640 | tf_op jit(solution)/shard_map/ppermute | solution.py:380
  156.3 9.1 %shard_map.168 = (bf16[512,768]{1,0:T(8,128)(2,1)}, bf16[128,768]{1,0:T(8,128)(2,1)}, bf16[128,768]{1,0:T(8,128)(2,1)}, bf16[128,768]{1,0:T(8,128)(2,1)}, bf16[128,768]{1,0:T(8,128)(2,1)}) custom-call(s32[3]{0:T(128)} %pad_add_fusion.sc, bf16[128,768]{1,0:T(8,128)(2,1)} %get-tuple-element.85.g0, bf16[128,768]{1,0:T(8,128)(2,1)} %copy-done.16, ...), custom_call_target="tpu_custom_call" | custom-call | flops 1811939328 | bytes 8388608 | tf_op jit(solution)/shard_map/pallas_call | solution.py:366
  182.4 4.6 shard_map.172
  191.4 39.6 %collective-permute-done.35.refs_6_ = bf16[128,1536]{1,0:T(8,128)(2,1)S(1)} collective-permute-done((bf16[128,1536]{1,0:T(8,128)(2,1)}, bf16[128,1536]{1,0:T(8,128)(2,1)S(1)}, u32[]{:S(2)}, u32[]{:S(2)}) %collective-permute-start.35) | collective-permute-done | bytes 393248 | tf_op jit(solution)/shard_map/ppermute | solution.py:380
  233.6 5.6 %shard_map.170 = (bf16[768,768]{1,0:T(8,128)(2,1)}, bf16[768,768]{1,0:T(8,128)(2,1)}) custom-call(bf16[128,1792]{1,0:T(8,128)(2,1)} %get-tuple-element.95.refs_0_.m0, bf16[128,1792]{1,0:T(8,128)(2,1)} %copy-done.19, bf16[128,1792]{1,0:T(8,128)(2,1)} %copy-done.20, bf16[128,1792]{1,0:T(8,128)(2,1)} %copy-done.21, ...), custom_call_target="tpu_custom_call" | custom-call | flops 1207959552 | bytes 8388608 | tf_op jit(solution)/shard_map/pallas_call | solution.py:366
  240.6 76.3 %all-reduce = f32[16,192]{1,0:T(8,128)S(1)} all-reduce(f32[16,192]{1,0:T(8,128)S(1)} %reshape.359), channel_id=2, replica_groups=mesh['section'=2,'dp'=4,'ctx'=4] {'dp','ctx'}, use_global_device_ids=true, to_apply=%region_0.1.clone | all-reduce | flops 3072 | bytes 24576
  320.7 5.0 %shard_map.173 = (bf16[768,768]{1,0:T(8,128)(2,1)}, bf16[192,768]{1,0:T(8,128)(2,1)}) custom-call(bf16[512,768]{1,0:T(8,128)(2,1)} %get-tuple-element.112.n1, bf16[512,768]{1,0:T(8,128)(2,1)} %get-tuple-element.113.gmixed, bf16[128,3328]{1,0:T(8,128)(2,1)} %get-tuple-element.104.refs_0_.m0, bf16[128,3328]{1,0:T(8,128)(2,1)} %copy-done.12, ...), custom_call_target="tpu_custom_call" | custom-call | flops 603979776 | bytes 8388608 | tf_op jit(solution)/shard_map/pallas_call | solution.py:366
  340.3 5.9 %shard_map.171 = (bf16[768,768]{1,0:T(8,128)(2,1)}, bf16[768,768]{1,0:T(8,128)(2,1)}) custom-call(bf16[128,3328]{1,0:T(8,128)(2,1)} %get-tuple-element.104.refs_0_.m0, bf16[128,3328]{1,0:T(8,128)(2,1)} %copy-done.12, bf16[128,3328]{1,0:T(8,128)(2,1)} %collective-permute-done.42.refs_2_.m2, bf16[128,3328]{1,0:T(8,128)(2,1)} %collective-permute-done.43.refs_3_.m3), custom_call_target="tpu_custom_call" | custom-call | flops 1207959552 | bytes 8388608 | tf_op jit(solution)/shard_map/pallas_call | solution.py:366
  350.0 8.6 %collective-permute-start.71 = (bf16[768,768]{1,0:T(8,128)(2,1)}, bf16[768,768]{1,0:T(8,128)(2,1)S(1)}, u32[]{:S(2)}, u32[]{:S(2)}) collective-permute-start(bf16[768,768]{1,0:T(8,128)(2,1)} %get-tuple-element.118), channel_id=1, source_target_pairs={{0,16},{1,17},{2,18},{3,19},{4,20},{5,21},{6,22},{7,23},{8,24},{9,... | collective-permute-start | bytes 3538952 | tf_op jit(solution)/shard_map/ppermute | solution.py:555
  366.8 4.9 %collective-permute-start.50 = (bf16[192,768]{1,0:T(8,128)(2,1)S(1)}, bf16[192,768]{1,0:T(8,128)(2,1)S(1)}, u32[]{:S(2)}, u32[]{:S(2)}) collective-permute-start(bf16[192,768]{1,0:T(8,128)(2,1)S(1)} %get-tuple-element.131), channel_id=1, source_target_pairs={{0,8},{4,12},{8,0},{12,4},{1,9},{5,13},{9,1},{13,5},{2,10},{6,14},... | collective-permute-start | bytes 884744 | tf_op jit(solution)/shard_map/ppermute | solution.py:422
  382.5 11.0 %collective-permute-done.50 = bf16[192,768]{1,0:T(8,128)(2,1)S(1)} collective-permute-done((bf16[192,768]{1,0:T(8,128)(2,1)S(1)}, bf16[192,768]{1,0:T(8,128)(2,1)S(1)}, u32[]{:S(2)}, u32[]{:S(2)}) %collective-permute-start.50) | collective-permute-done | bytes 294944 | tf_op jit(solution)/shard_map/ppermute | solution.py:422
  394.2 6.1 %collective-permute-done.51 = bf16[192,768]{1,0:T(8,128)(2,1)S(1)} collective-permute-done((bf16[192,768]{1,0:T(8,128)(2,1)S(1)}, bf16[192,768]{1,0:T(8,128)(2,1)S(1)}, u32[]{:S(2)}, u32[]{:S(2)}) %collective-permute-start.51) | collective-permute-done | bytes 294944 | tf_op jit(solution)/shard_map/ppermute | solution.py:422
  401.3 10.2 %collective-permute-start.39 = (bf16[192,768]{1,0:T(8,128)(2,1)S(1)}, bf16[192,768]{1,0:T(8,128)(2,1)S(1)}, u32[]{:S(2)}, u32[]{:S(2)}) collective-permute-start(bf16[192,768]{1,0:T(8,128)(2,1)S(1)} %get-tuple-element.137), channel_id=1, source_target_pairs={{0,8},{4,12},{8,0},{12,4},{1,9},{5,13},{9,1},{13,5},{2,10},{6,14},... | collective-permute-start | bytes 884744 | tf_op jit(solution)/shard_map/ppermute | solution.py:422
  411.6 5.3 %collective-permute-start.40 = (bf16[192,768]{1,0:T(8,128)(2,1)S(1)}, bf16[192,768]{1,0:T(8,128)(2,1)S(1)}, u32[]{:S(2)}, u32[]{:S(2)}) collective-permute-start(bf16[192,768]{1,0:T(8,128)(2,1)S(1)} %get-tuple-element.136), channel_id=1, source_target_pairs={{0,12},{4,0},{8,4},{12,8},{1,13},{5,1},{9,5},{13,9},{2,14},{6,2},{... | collective-permute-start | bytes 884744 | tf_op jit(solution)/shard_map/ppermute | solution.py:422
  419.3 8.1 %collective-permute-done.39 = bf16[192,768]{1,0:T(8,128)(2,1)S(1)} collective-permute-done((bf16[192,768]{1,0:T(8,128)(2,1)S(1)}, bf16[192,768]{1,0:T(8,128)(2,1)S(1)}, u32[]{:S(2)}, u32[]{:S(2)}) %collective-permute-start.39) | collective-permute-done | bytes 294944 | tf_op jit(solution)/shard_map/ppermute | solution.py:422
  429.3 9.3 %collective-permute-start.70 = (bf16[192,768]{1,0:T(8,128)(2,1)S(1)}, bf16[192,768]{1,0:T(8,128)(2,1)S(1)}, u32[]{:S(2)}, u32[]{:S(2)}) collective-permute-start(bf16[192,768]{1,0:T(8,128)(2,1)S(1)} %get-tuple-element.124), channel_id=1, source_target_pairs={{0,12},{4,0},{8,4},{12,8},{1,13},{5,1},{9,5},{13,9},{2,14},{6,2},{... | collective-permute-start | bytes 884744 | tf_op jit(solution)/shard_map/ppermute | solution.py:422
  (316 shorter events, 179.2 us)
Async XLA Ops:
  0.6 48.1 %collective-permute-start.10 = (bf16[3072,768]{1,0:T(8,128)(2,1)}, bf16[3072,768]{1,0:T(8,128)(2,1)}, u32[]{:S(2)}, u32[]{:S(2)}) collective-permute-start(bf16[3072,768]{1,0:T(8,128)(2,1)} %bitcast.194), channel_id=1, source_target_pairs={{0,16},{16,0},{1,17},{17,1},{2,18},{18,2},{3,19},{19,3},{4,20},{20... | collective-permute-start | bytes 14155784 | tf_op jit(solution)/shard_map/ppermute | solution.py:385
  1.2 47.6 %collective-permute-start.9 = (bf16[768,3072]{1,0:T(8,128)(2,1)}, bf16[768,3072]{1,0:T(8,128)(2,1)}, u32[]{:S(2)}, u32[]{:S(2)}) collective-permute-start(bf16[768,3072]{1,0:T(8,128)(2,1)} %bitcast.190), channel_id=1, source_target_pairs={{0,16},{16,0},{1,17},{17,1},{2,18},{18,2},{3,19},{19,3},{4,20},{20... | collective-permute-start | bytes 14155784 | tf_op jit(solution)/shard_map/ppermute | solution.py:385
  6.7 24.9 %collective-permute-start.4 = (bf16[768,768]{1,0:T(8,128)(2,1)}, bf16[768,768]{1,0:T(8,128)(2,1)S(1)}, u32[]{:S(2)}, u32[]{:S(2)}) collective-permute-start(bf16[768,768]{1,0:T(8,128)(2,1)} %fusion.6.w_own), channel_id=1, source_target_pairs={{0,16},{16,0},{1,17},{17,1},{2,18},{18,2},{3,19},{19,3},{4,20},{20... | collective-permute-start | bytes 3538952 | tf_op jit(solution)/shard_map/ppermute | solution.py:385
  7.2 36.2 %collective-permute-start.8 = (bf16[768,768]{1,0:T(8,128)(2,1)}, bf16[768,768]{1,0:T(8,128)(2,1)S(1)}, u32[]{:S(2)}, u32[]{:S(2)}) collective-permute-start(bf16[768,768]{1,0:T(8,128)(2,1)} %bitcast.7.wo_own), channel_id=1, source_target_pairs={{0,16},{16,0},{1,17},{17,1},{2,18},{18,2},{3,19},{19,3},{4,20},{20... | collective-permute-start | bytes 3538952 | tf_op jit(solution)/shard_map/ppermute | solution.py:385
  133.5 33.1 %collective-permute-start.31 = (bf16[128,1792]{1,0:T(8,128)(2,1)S(1)}, bf16[128,1792]{1,0:T(8,128)(2,1)S(1)}, u32[]{:S(2)}, u32[]{:S(2)}) collective-permute-start(bf16[128,1792]{1,0:T(8,128)(2,1)S(1)} %copy-done.47), channel_id=1, source_target_pairs={{0,1},{1,0},{2,3},{3,2},{4,5},{5,4},{6,7},{7,6},{8,9},{9,8},{10,11... | collective-permute-start | bytes 1376264 | tf_op jit(solution)/shard_map/ppermute | solution.py:380
  134.9 33.0 %collective-permute-start.32 = (bf16[128,1792]{1,0:T(8,128)(2,1)S(1)}, bf16[128,1792]{1,0:T(8,128)(2,1)S(1)}, u32[]{:S(2)}, u32[]{:S(2)}) collective-permute-start(bf16[128,1792]{1,0:T(8,128)(2,1)S(1)} %copy-done.46), channel_id=1, source_target_pairs={{0,2},{1,3},{2,0},{3,1},{4,6},{5,7},{6,4},{7,5},{8,10},{9,11},{10,... | collective-permute-start | bytes 1376264 | tf_op jit(solution)/shard_map/ppermute | solution.py:380
  136.2 34.2 %collective-permute-start.33 = (bf16[128,1792]{1,0:T(8,128)(2,1)S(1)}, bf16[128,1792]{1,0:T(8,128)(2,1)S(1)}, u32[]{:S(2)}, u32[]{:S(2)}) collective-permute-start(bf16[128,1792]{1,0:T(8,128)(2,1)S(1)} %copy-done.45), channel_id=1, source_target_pairs={{0,3},{1,2},{2,1},{3,0},{4,7},{5,6},{6,5},{7,4},{8,11},{9,10},{10,... | collective-permute-start | bytes 1376264 | tf_op jit(solution)/shard_map/ppermute | solution.py:380
  155.3 24.2 %collective-permute-start.34 = (bf16[128,1536]{1,0:T(8,128)(2,1)}, bf16[128,1536]{1,0:T(8,128)(2,1)}, u32[]{:S(2)}, u32[]{:S(2)}) collective-permute-start(bf16[128,1536]{1,0:T(8,128)(2,1)} %get-tuple-element.100), channel_id=1, source_target_pairs={{0,1},{1,0},{2,3},{3,2},{4,5},{5,4},{6,7},{7,6},{8,9},{9,8},{10,11... | collective-permute-start | bytes 1179656 | tf_op jit(solution)/shard_map/ppermute | solution.py:380
  170.4 147.7 %collective-permute-start.41 = (bf16[128,3328]{1,0:T(8,128)(2,1)}, bf16[128,3328]{1,0:T(8,128)(2,1)S(1)}, u32[]{:S(2)}, u32[]{:S(2)}) collective-permute-start(bf16[128,3328]{1,0:T(8,128)(2,1)} %get-tuple-element.105), channel_id=1, source_target_pairs={{0,1},{1,0},{2,3},{3,2},{4,5},{5,4},{6,7},{7,6},{8,9},{9,8},{10,11... | collective-permute-start | bytes 2555912 | tf_op jit(solution)/shard_map/ppermute | solution.py:380
  173.4 146.0 %collective-permute-start.42 = (bf16[128,3328]{1,0:T(8,128)(2,1)}, bf16[128,3328]{1,0:T(8,128)(2,1)}, u32[]{:S(2)}, u32[]{:S(2)}) collective-permute-start(bf16[128,3328]{1,0:T(8,128)(2,1)} %get-tuple-element.106), channel_id=1, source_target_pairs={{0,2},{1,3},{2,0},{3,1},{4,6},{5,7},{6,4},{7,5},{8,10},{9,11},{10,... | collective-permute-start | bytes 2555912 | tf_op jit(solution)/shard_map/ppermute | solution.py:380
  177.3 143.3 %collective-permute-start.43 = (bf16[128,3328]{1,0:T(8,128)(2,1)}, bf16[128,3328]{1,0:T(8,128)(2,1)}, u32[]{:S(2)}, u32[]{:S(2)}) collective-permute-start(bf16[128,3328]{1,0:T(8,128)(2,1)} %get-tuple-element.107), channel_id=1, source_target_pairs={{0,3},{1,2},{2,1},{3,0},{4,7},{5,6},{6,5},{7,4},{8,11},{9,10},{10,... | collective-permute-start | bytes 2555912 | tf_op jit(solution)/shard_map/ppermute | solution.py:380
  179.5 51.5 %collective-permute-start.35 = (bf16[128,1536]{1,0:T(8,128)(2,1)}, bf16[128,1536]{1,0:T(8,128)(2,1)S(1)}, u32[]{:S(2)}, u32[]{:S(2)}) collective-permute-start(bf16[128,1536]{1,0:T(8,128)(2,1)} %get-tuple-element.101), channel_id=1, source_target_pairs={{0,2},{1,3},{2,0},{3,1},{4,6},{5,7},{6,4},{7,5},{8,10},{9,11},{10,... | collective-permute-start | bytes 1179656 | tf_op jit(solution)/shard_map/ppermute | solution.py:380
  179.6 52.8 %collective-permute-start.36 = (bf16[128,1536]{1,0:T(8,128)(2,1)}, bf16[128,1536]{1,0:T(8,128)(2,1)S(1)}, u32[]{:S(2)}, u32[]{:S(2)}) collective-permute-start(bf16[128,1536]{1,0:T(8,128)(2,1)} %get-tuple-element.102), channel_id=1, source_target_pairs={{0,3},{1,2},{2,1},{3,0},{4,7},{5,6},{6,5},{7,4},{8,11},{9,10},{10,... | collective-permute-start | bytes 1179656 | tf_op jit(solution)/shard_map/ppermute | solution.py:380
  231.0 96.6 %collective-permute-start.59 = (bf16[192,768]{1,0:T(8,128)(2,1)}, bf16[192,768]{1,0:T(8,128)(2,1)S(1)}, u32[]{:S(2)}, u32[]{:S(2)}) collective-permute-start(bf16[192,768]{1,0:T(8,128)(2,1)} %get-tuple-element.115), channel_id=1, source_target_pairs={{16,0},{17,1},{18,2},{19,3},{20,4},{21,5},{22,6},{23,7},{24,8},{25... | collective-permute-start | bytes 884744 | tf_op jit(solution)/shard_map/ppermute | solution.py:555
  239.2 121.7 %collective-permute-start.48 = (bf16[768,768]{1,0:T(8,128)(2,1)S(1)}, bf16[768,768]{1,0:T(8,128)(2,1)}, u32[]{:S(2)}, u32[]{:S(2)}) collective-permute-start(bf16[768,768]{1,0:T(8,128)(2,1)S(1)} %copy-done.6), channel_id=1, source_target_pairs={{16,0},{17,1},{18,2},{19,3},{20,4},{21,5},{22,6},{23,7},{24,8},{25... | collective-permute-start | bytes 3538952 | tf_op jit(solution)/shard_map/ppermute | solution.py:555
  318.1 45.9 %collective-permute-start.67 = (bf16[768,768]{1,0:T(8,128)(2,1)}, bf16[768,768]{1,0:T(8,128)(2,1)S(1)}, u32[]{:S(2)}, u32[]{:S(2)}) collective-permute-start(bf16[768,768]{1,0:T(8,128)(2,1)} %get-tuple-element.117), channel_id=1, source_target_pairs={{16,0},{17,1},{18,2},{19,3},{20,4},{21,5},{22,6},{23,7},{24,8},{25... | collective-permute-start | bytes 3538952 | tf_op jit(solution)/shard_map/ppermute | solution.py:555
  319.4 28.2 %collective-permute-start.30 = (f32[128,768]{1,0:T(8,128)S(1)}, f32[128,768]{1,0:T(8,128)S(1)}, u32[]{:S(2)}, u32[]{:S(2)}) collective-permute-start(f32[128,768]{1,0:T(8,128)S(1)} %get-tuple-element.144), channel_id=1, source_target_pairs={{0,16},{16,0},{1,17},{17,1},{2,18},{18,2},{3,19},{19,3},{4,20},{20... | collective-permute-start | bytes 1179656 | tf_op jit(solution)/shard_map/ppermute | solution.py:385
  350.0 28.9 %collective-permute-start.71 = (bf16[768,768]{1,0:T(8,128)(2,1)}, bf16[768,768]{1,0:T(8,128)(2,1)S(1)}, u32[]{:S(2)}, u32[]{:S(2)}) collective-permute-start(bf16[768,768]{1,0:T(8,128)(2,1)} %get-tuple-element.118), channel_id=1, source_target_pairs={{0,16},{1,17},{2,18},{3,19},{4,20},{5,21},{6,22},{7,23},{8,24},{9,... | collective-permute-start | bytes 3538952 | tf_op jit(solution)/shard_map/ppermute | solution.py:555
  366.8 26.8 %collective-permute-start.50 = (bf16[192,768]{1,0:T(8,128)(2,1)S(1)}, bf16[192,768]{1,0:T(8,128)(2,1)S(1)}, u32[]{:S(2)}, u32[]{:S(2)}) collective-permute-start(bf16[192,768]{1,0:T(8,128)(2,1)S(1)} %get-tuple-element.131), channel_id=1, source_target_pairs={{0,8},{4,12},{8,0},{12,4},{1,9},{5,13},{9,1},{13,5},{2,10},{6,14},... | collective-permute-start | bytes 884744 | tf_op jit(solution)/shard_map/ppermute | solution.py:422
  372.2 28.1 %collective-permute-start.51 = (bf16[192,768]{1,0:T(8,128)(2,1)S(1)}, bf16[192,768]{1,0:T(8,128)(2,1)S(1)}, u32[]{:S(2)}, u32[]{:S(2)}) collective-permute-start(bf16[192,768]{1,0:T(8,128)(2,1)S(1)} %get-tuple-element.130), channel_id=1, source_target_pairs={{0,12},{4,0},{8,4},{12,8},{1,13},{5,1},{9,5},{13,9},{2,14},{6,2},{... | collective-permute-start | bytes 884744 | tf_op jit(solution)/shard_map/ppermute | solution.py:422
  374.8 26.5 %collective-permute-start.68 = (bf16[192,768]{1,0:T(8,128)(2,1)S(1)}, bf16[192,768]{1,0:T(8,128)(2,1)S(1)}, u32[]{:S(2)}, u32[]{:S(2)}) collective-permute-start(bf16[192,768]{1,0:T(8,128)(2,1)S(1)} %get-tuple-element.123), channel_id=1, source_target_pairs={{0,4},{4,8},{8,12},{12,0},{1,5},{5,9},{9,13},{13,1},{2,6},{6,10},{... | collective-permute-start | bytes 884744 | tf_op jit(solution)/shard_map/ppermute | solution.py:422
  378.9 32.7 %collective-permute-start.38 = (bf16[192,768]{1,0:T(8,128)(2,1)S(1)}, bf16[192,768]{1,0:T(8,128)(2,1)S(1)}, u32[]{:S(2)}, u32[]{:S(2)}) collective-permute-start(bf16[192,768]{1,0:T(8,128)(2,1)S(1)} %get-tuple-element.135), channel_id=1, source_target_pairs={{0,4},{4,8},{8,12},{12,0},{1,5},{5,9},{9,13},{13,1},{2,6},{6,10},{... | collective-permute-start | bytes 884744 | tf_op jit(solution)/shard_map/ppermute | solution.py:422
  381.8 35.1 %collective-permute-start.53 = (bf16[192,768]{1,0:T(8,128)(2,1)S(1)}, bf16[192,768]{1,0:T(8,128)(2,1)S(1)}, u32[]{:S(2)}, u32[]{:S(2)}) collective-permute-start(bf16[192,768]{1,0:T(8,128)(2,1)S(1)} %get-tuple-element.132), channel_id=1, source_target_pairs={{16,20},{20,24},{24,28},{28,16},{17,21},{21,25},{25,29},{29,17},{1... | collective-permute-start | bytes 884744 | tf_op jit(solution)/shard_map/ppermute | solution.py:422
  401.3 26.1 %collective-permute-start.39 = (bf16[192,768]{1,0:T(8,128)(2,1)S(1)}, bf16[192,768]{1,0:T(8,128)(2,1)S(1)}, u32[]{:S(2)}, u32[]{:S(2)}) collective-permute-start(bf16[192,768]{1,0:T(8,128)(2,1)S(1)} %get-tuple-element.137), channel_id=1, source_target_pairs={{0,8},{4,12},{8,0},{12,4},{1,9},{5,13},{9,1},{13,5},{2,10},{6,14},... | collective-permute-start | bytes 884744 | tf_op jit(solution)/shard_map/ppermute | solution.py:422
  (109 other events, 1030.2 us)
